TPU v7x, 32 devices: a whole 2x2x4 slice. The times are simulated.
32 devices in a mesh: grp: 2 (over y), tok: 4 (over z), tp: 4 (over x, core).
Axes of the slice: x: 2, y: 2, z: 4, core: 2. Of those that a mesh axis runs over, the one named last changes fastest.
Arguments:
- inputs: bfloat16 [256, 8192], P(('grp', 'tok'), 'tp'), parts along dimension 0, may hold values from -6 to 6
- gate_weight: bfloat16 [8192, 16384], P('tp', 'tok'), may hold values from -0.0625 to 0.0625
- up_weight: bfloat16 [8192, 16384], P('tp', 'tok'), may hold values from -0.0625 to 0.0625
- down_weight: bfloat16 [16384, 4096], P('tok', 'tp'), may hold values from -0.046875 to 0.046875
Outputs:
- gram: float32 [8192, 4096], P(('grp', 'tok'), 'tp'), parts along dimension 0
- cross: float32 [8192, 4096], P(('grp', 'tok'), 'tp'), parts along dimension 0
There are 2 independent parts, one for each index of `grp`. A program takes and returns all parts, laid end to end along the dimension named above; an argument that names none is the same for every part. Nothing has to cross between parts.
All inputs are finite; a program needn't handle non-finite values.
Results may differ from a plain program's by a relative error of at most 0.02.
Values may be sent and summed in bfloat16 or wider, within the bound.
A program may use at most 192 MiB of HBM per device.

v0:
```python
import jax
import jax.numpy as jnp
from jax import lax
from jax.sharding import PartitionSpec as P

WIN = 4096


def fold_parts(received, owners):
    rows = received.shape[0] // owners
    return received.astype(jnp.float32).reshape(owners, rows, received.shape[1]).sum(axis=0)


def shards(inputs, gate_weight, up_weight, down_weight):
    width_tp = lax.axis_size("tp")
    width_tok = lax.axis_size("tok")
    share = lax.axis_index("tp")
    full_rows = lax.all_gather(inputs, "tp", axis=1, tiled=True)
    window = full_rows[:, :WIN]
    columns = WIN // width_tp
    own_cols = lax.dynamic_slice_in_dim(window, share * columns, columns, 1)
    every_token = lax.all_gather(inputs, "tok", axis=0, tiled=True)
    gate_part = jnp.dot(every_token, gate_weight, preferred_element_type=jnp.float32)
    up_part = jnp.dot(every_token, up_weight, preferred_element_type=jnp.float32)
    both = lax.psum_scatter(
        jnp.concatenate([gate_part, up_part], axis=1).astype(jnp.bfloat16),
        "tp",
        scatter_dimension=0,
        tiled=True,
    ).astype(jnp.float32)
    half = gate_weight.shape[1]
    hidden = (jax.nn.silu(both[:, :half]) * both[:, half:]).astype(jnp.bfloat16)
    terms = jnp.dot(
        lax.all_gather(hidden, "tp", axis=0, tiled=True),
        down_weight,
        preferred_element_type=jnp.float32,
    )
    target = lax.psum_scatter(terms.astype(jnp.bfloat16), "tok", scatter_dimension=0, tiled=True)
    cross_part = jnp.dot(window.T, target, preferred_element_type=jnp.float32).astype(jnp.bfloat16)
    gram_part = jnp.dot(window.T, own_cols, preferred_element_type=jnp.float32).astype(jnp.bfloat16)
    gram_recv, cross_recv = (
        lax.all_to_all(gram_part, "tok", split_axis=0, concat_axis=0, tiled=True),
        lax.all_to_all(cross_part, "tok", split_axis=0, concat_axis=0, tiled=True),
    )
    return (fold_parts(gram_recv, width_tok), fold_parts(cross_recv, width_tok))


def solution(mesh):
    placed = (P(("grp", "tok"), "tp"), P("tp", "tok"), P("tp", "tok"), P("tok", "tp"))
    return jax.shard_map(
        shards,
        mesh=mesh,
        in_specs=placed,
        out_specs=(P(("grp", "tok"), "tp"), P(("grp", "tok"), "tp")),
        check_vma=False,
    )
```

profile of v0, /device:TPU:0, one launch (start us, length us, event | category | flops | bytes accessed | tf_op | source)
XLA Modules:
  0.0 545.3 jit_solution(16630438037162614458)
XLA Ops:
  7.2 8.8 %all_gather.9 = bf16[32,8192]{1,0:T(8,128)(2,1)S(1)} all-gather(bf16[32,2048]{1,0:T(8,128)(2,1)} %param.4), channel_id=1, replica_groups=mesh['grp'=2,'tok'=4,'tp'=4] {'tp'}, dimensions={1}, use_global_device_ids=true | all-gather | bytes 655360 | tf_op jit(solution)/shard_map/all_gather | solution.py:18
  16.0 5.6 %convolution_convert_fusion.1 = bf16[1024,4096]{1,0:T(8,128)(2,1)} fusion(bf16[32,4096]{1,0:T(8,128)(2,1)S(1)} %slice.12, s32[]{:T(128)S(6)} %select_n.3), kind=kOutput, calls=%fused_computation.5 | convolution fusion | flops 272629760 | bytes 8716292 | tf_op jit(solution)/shard_map/dot_general | solution.py:40
  21.6 7.9 %copy.19 = bf16[128,4,8,1024]{3,2,0,1:T(8,128)(2,1)} copy(bf16[128,4,8,1024]{3,2,1,0:T(8,128)(2,1)} %bitcast.18) | data formatting | bytes 16777216 | tf_op jit(solution)/shard_map/all_to_all | solution.py:42
  29.6 5.8 %all-to-all-start = ((bf16[4,1024,1024]{1,2,0:T(8,128)(2,1)}), bf16[4,1024,1024]{1,2,0:T(8,128)(2,1)}, u32[]{:S(2)}, u32[]{:S(2)}) async-start(bf16[4,1024,1024]{1,2,0:T(8,128)(2,1)} %bitcast.20), calls=%async_computation | async-start | bytes 16777216 | tf_op jit(solution)/shard_map/all_to_all | solution.py:42
  35.4 193.9 %all_gather.10 = bf16[128,2048]{1,0:T(8,128)(2,1)S(1)} all-gather(bf16[32,2048]{1,0:T(8,128)(2,1)S(1)} %copy-done), channel_id=1, replica_groups=mesh['grp'=2,'tok'=4,'tp'=4] {'tok'}, dimensions={0}, use_global_device_ids=true | all-gather | bytes 655360 | tf_op jit(solution)/shard_map/all_gather | solution.py:22
  229.3 8.1 %convolution_convert_fusion.2 = bf16[128,4096]{1,0:T(8,128)(2,1)S(1)} fusion(bf16[128,2048]{1,0:T(8,128)(2,1)S(1)} %all_gather.10, bf16[2048,4096]{1,0:T(8,128)(2,1)} %param.6), kind=kOutput, calls=%fused_computation.6 | convolution fusion | flops 2148007936 | bytes 18350080 | tf_op jit(solution)/shard_map/dot_general | solution.py:24
  237.5 8.1 %convolution_convert_fusion.3 = bf16[128,4096]{1,0:T(8,128)(2,1)S(1)} fusion(bf16[128,2048]{1,0:T(8,128)(2,1)S(1)} %all_gather.10, bf16[2048,4096]{1,0:T(8,128)(2,1)} %param.5), kind=kOutput, calls=%fused_computation.7 | convolution fusion | flops 2148007936 | bytes 18350080 | tf_op jit(solution)/shard_map/dot_general | solution.py:23
  245.6 1.5 pad_maximum_fusion
  247.1 0.0 all-gather.2.cloned.1.call-start
  247.2 32.2 %reduce-scatter.3.cloned.1.call-done = bf16[32,8192]{1,0:T(8,128)(2,1)} async-done(((bf16[128,8192]{1,0:T(8,128)(2,1)}), bf16[32,8192]{1,0:T(8,128)(2,1)}) %reduce-scatter.3.cloned.1.call-update) | async-done | bytes 524304 | tf_op jit(solution)/shard_map/reduce_scatter | solution.py:25
  279.4 1.1 convert_element_type.33
  280.5 0.8 fusion
  281.3 0.2 reduce-scatter.5.cloned.1.call-start
  281.6 16.7 %all-gather.2.cloned.1.call-done = bf16[128,4096]{1,0:T(8,128)(2,1)} async-done(((bf16[32,4096]{1,0:T(8,128)(2,1)}), bf16[128,4096]{1,0:T(8,128)(2,1)}) %all-gather.2.cloned.1.call-update) | async-done | bytes 1048592 | tf_op jit(solution)/shard_map/all_gather | solution.py:34
  298.3 5.7 %convolution_convert_fusion.4 = bf16[128,1024]{1,0:T(8,128)(2,1)} fusion(bf16[128,4096]{1,0:T(8,128)(2,1)} %all-gather.2.cloned.1.call-done, bf16[4096,1024]{1,0:T(8,128)(2,1)} %param.7), kind=kOutput, calls=%fused_computation.9 | convolution fusion | flops 1073872896 | bytes 9699328 | tf_op jit(solution)/shard_map/dot_general | solution.py:33
  304.0 19.8 %reduce-scatter.5.cloned.1.call-done = bf16[32,1024]{1,0:T(8,128)(2,1)} async-done(((bf16[128,1024]{1,0:T(8,128)(2,1)}), bf16[32,1024]{1,0:T(8,128)(2,1)}) %reduce-scatter.5.cloned.1.call-update) | async-done | bytes 65552 | tf_op jit(solution)/shard_map/reduce_scatter | solution.py:38
  323.8 6.4 %convolution_convert_fusion = bf16[1024,4096]{1,0:T(8,128)(2,1)} fusion(bf16[32,1024]{1,0:T(8,128)(2,1)} %reduce-scatter.5.cloned.1.call-done, bf16[32,8192]{1,0:T(8,128)(2,1)S(1)} %all_gather.9), kind=kOutput, calls=%fused_computation.4 | convolution fusion | flops 272629760 | bytes 8716288 | tf_op jit(solution)/shard_map/dot_general | solution.py:39
  330.2 7.9 %copy.18 = bf16[128,4,8,1024]{3,2,0,1:T(8,128)(2,1)} copy(bf16[128,4,8,1024]{3,2,1,0:T(8,128)(2,1)} %bitcast.19) | data formatting | bytes 16777216 | tf_op jit(solution)/shard_map/all_to_all | solution.py:43
  338.2 5.7 %all-to-all-start.1 = ((bf16[4,1024,1024]{1,2,0:T(8,128)(2,1)}), bf16[4,1024,1024]{1,2,0:T(8,128)(2,1)}, u32[]{:S(2)}, u32[]{:S(2)}) async-start(bf16[4,1024,1024]{1,2,0:T(8,128)(2,1)} %bitcast.21), calls=%async_computation.3 | async-start | bytes 16777216 | tf_op jit(solution)/shard_map/all_to_all | solution.py:43
  343.9 7.9 %convert_reduce_fusion.1 = f32[1024,1024]{0,1:T(8,128)} fusion(bf16[4,1024,1024]{1,2,0:T(8,128)(2,1)} %all-to-all-done), kind=kLoop, calls=%fused_computation.1 | loop fusion | flops 7340032 | bytes 12582912 | tf_op jit(solution)/shard_map/reduce_sum | solution.py:11
  351.8 5.3 copy.10
  357.1 168.5 %all-to-all-done.1 = bf16[4,1024,1024]{1,2,0:T(8,128)(2,1)} async-done(((bf16[4,1024,1024]{1,2,0:T(8,128)(2,1)}), bf16[4,1024,1024]{1,2,0:T(8,128)(2,1)}, u32[]{:S(2)}, u32[]{:S(2)}) %all-to-all-start.1) | async-done | bytes 8388640 | tf_op jit(solution)/shard_map/all_to_all | solution.py:43
  525.6 7.9 %convert_reduce_fusion = f32[1024,1024]{0,1:T(8,128)} fusion(bf16[4,1024,1024]{1,2,0:T(8,128)(2,1)} %all-to-all-done.1), kind=kLoop, calls=%fused_computation | loop fusion | flops 7340032 | bytes 12582912 | tf_op jit(solution)/shard_map/reduce_sum | solution.py:11
  533.5 5.3 copy.11
  (8 shorter events, 0.1 us)
Async XLA Ops:
  29.6 5.8 %copy-start = (bf16[32,2048]{1,0:T(8,128)(2,1)S(1)}, bf16[32,2048]{1,0:T(8,128)(2,1)}, u32[]{:S(2)}) copy-start(bf16[32,2048]{1,0:T(8,128)(2,1)} %param.4) | copy-start | bytes 393220
  29.6 308.6 %all-to-all-start = ((bf16[4,1024,1024]{1,2,0:T(8,128)(2,1)}), bf16[4,1024,1024]{1,2,0:T(8,128)(2,1)}, u32[]{:S(2)}, u32[]{:S(2)}) async-start(bf16[4,1024,1024]{1,2,0:T(8,128)(2,1)} %bitcast.20), calls=%async_computation | async-start | bytes 16777216 | tf_op jit(solution)/shard_map/all_to_all | solution.py:42
  35.3 244.0 %reduce-scatter.3.cloned.1.call-start = ((), (), s32[]{:S(2)}) async-start(), calls=%async_computation.4 | async-start | bytes 2621440 | tf_op jit(solution)/shard_map/reduce_scatter | solution.py:25
  247.1 51.2 %all-gather.2.cloned.1.call-start = ((), (), s32[]{:S(2)}) async-start(), calls=%async_computation.5 | async-start | bytes 1310720 | tf_op jit(solution)/shard_map/all_gather | solution.py:34
  281.3 42.5 %reduce-scatter.5.cloned.1.call-start = ((), (), s32[]{:S(2)}) async-start(), calls=%async_computation.6 | async-start | bytes 327680 | tf_op jit(solution)/shard_map/reduce_scatter | solution.py:38
  338.2 187.4 %all-to-all-start.1 = ((bf16[4,1024,1024]{1,2,0:T(8,128)(2,1)}), bf16[4,1024,1024]{1,2,0:T(8,128)(2,1)}, u32[]{:S(2)}, u32[]{:S(2)}) async-start(bf16[4,1024,1024]{1,2,0:T(8,128)(2,1)} %bitcast.21), calls=%async_computation.3 | async-start | bytes 16777216 | tf_op jit(solution)/shard_map/all_to_all | solution.py:43
Sparse Core Ops, SparseCore 0:
  247.2 32.0 reduce-scatter.2
  281.6 16.7 all-gather.1
  304.1 19.6 reduce-scatter.4
where the time goes:
time: 546 us; the launch traced here: 545 us
  waiting for transfers between devices  237 us (43%)
  blocking collectives  203 us (37%)
  matrix products  34 us (6%)
  local copies, waits for them, and re-layouts  26.6 us (5%)
  other arithmetic  19.2 us (4%)
  between operations  13.8 us (3%)
  starting transfers between devices  11.7 us (2%)
    all_gather x1, blocking collectives, shards(): every_token = lax.all_gather(inputs, 'tok', axis=0, tiled=True)  194 us
    all_to_all x1, waiting for transfers between devices, shards(): lax.all_to_all(cross_part, 'tok', split_axis=0, concat_axis=0, tiled=True)  168 us
    reduce_scatter x1, waiting for transfers between devices, shards(): lax.psum_scatter(jnp.concatenate([gate_part, up_part], axis=1).astype(jnp...  32.2 us
    reduce_scatter x1, waiting for transfers between devices, shards(): lax.psum_scatter(terms.astype(jnp.bfloat16), 'tok', scatter_dimension=0,...  19.8 us
    all_gather x1, waiting for transfers between devices, shards(): lax.all_gather(hidden, 'tp', axis=0, tiled=True)  16.7 us
    reduce_sum x2, other arithmetic, fold_parts(): received.astype(jnp.float32).reshape(owners, rows, received.shape[1])  15.8 us
  transfers between devices with their start and end apart: 5, of which 4 were waited for; matrix products, arithmetic and copies ran while one was open for 10% of the time, Pallas kernels for 0%

commit v1 on v0

v1 whole, which is shorter than its diff:
```python
import functools

import jax
import jax.numpy as jnp
from jax import lax
from jax.experimental import pallas as pl
from jax.experimental.pallas import tpu as pltpu
from jax.sharding import PartitionSpec as P

WIN = 4096
CHUNK = 512
MESH = pl.DeviceIdType.MESH
F32 = jnp.float32
BF16 = jnp.bfloat16


def span_kernel(
    n_tok, n_tp,
    x_ref, gate_ref, up_ref, down_ref,
    tgt_ref, wrow_ref, wcol_ref,
    xg, wg, wd, part, r1, s1, r2, hid, acc, ts, tr, tg, wr, wc,
    ld_x, ld_w, ld_d, gs, gr, c1s, c1r, x1s, x1r, x2s, x2r, c2s, c2r,
    zs, zr, bs, br, wrs, wrr, wcs, wcr,
):
    t = lax.axis_index("tok")
    p = lax.axis_index("tp")
    core = lax.rem(p, 2)
    x = p // 2
    n_x = n_tp // 2
    nc, _, feats, w = wg.shape
    rows = xg.shape[1]
    m = n_tok * rows
    b = m // n_tp
    win_rows, win_cols = wr.shape[2], wc.shape[2]

    def tok_peer(k):
        return lax.rem(t + k, n_tok)

    def x_peer(k):
        return lax.rem(x + k, n_x)

    def remote(src, dst, ssem, rsem, **where):
        return pltpu.make_async_remote_copy(
            src_ref=src, dst_ref=dst, send_sem=ssem, recv_sem=rsem,
            device_id=where, device_id_type=MESH,
        )

    partner = p + 1 - 2 * core

    own_x = pltpu.make_async_copy(x_ref, xg.at[t], ld_x)
    own_x.start()

    def load_w(c, j):
        src = (gate_ref, up_ref)[j]
        cols = pl.ds(pl.multiple_of(c * w, w), w)
        return pltpu.make_async_copy(src.at[:, cols], wg.at[c, j], ld_w.at[c, j])

    def load_d(c):
        return pltpu.make_async_copy(
            down_ref.at[pl.ds(pl.multiple_of(c * w, w), w), :], wd.at[c], ld_d.at[c]
        )

    @pl.loop(0, nc)
    def _(c):
        load_w(c, 0).start()
        load_w(c, 1).start()

    @pl.loop(0, nc)
    def _(c):
        load_d(c).start()

    barrier = pltpu.get_barrier_semaphore()
    for k in range(1, n_tok):
        pl.semaphore_signal(barrier, inc=1, device_id={"tok": tok_peer(k)}, device_id_type=MESH)
    for k in range(1, n_tp):
        pl.semaphore_signal(barrier, inc=1, device_id={"tp": lax.rem(p + k, n_tp)}, device_id_type=MESH)
    pl.semaphore_wait(barrier, n_tok + n_tp - 2)

    def gather(k):
        to = tok_peer(k)
        return remote(x_ref, xg.at[t], gs.at[to], gr.at[t], tok=to)

    def gathered(k):
        src = tok_peer(k)
        return remote(x_ref, xg.at[src], gs.at[src], gr.at[src], tok=src)

    for k in range(1, n_tok):
        gather(k).start()
    own_x.wait()
    for k in range(1, n_tok):
        gathered(k).wait_recv()

    def core_sum(c):
        return remote(part.at[c, 1 - core], r1.at[c], c1s.at[c], c1r.at[c], tp=partner)

    def x_sum(c, k):
        to = x_peer(k)
        return remote(s1.at[c, to], r2.at[c, x], x1s.at[c, to], x1r.at[c, x], tp=2 * to + core)

    def x_summed(c, k):
        src = x_peer(k)
        return remote(s1.at[c, src], r2.at[c, src], x1s.at[c, src], x1r.at[c, src], tp=2 * src + core)

    def x_hid(c, k):
        to = x_peer(k)
        mine = hid.at[c, core * n_x + x]
        return remote(mine, mine, x2s.at[c, to], x2r.at[c, x], tp=2 * to + core)

    def x_hidden(c, k):
        src = x_peer(k)
        theirs = hid.at[c, core * n_x + src]
        return remote(theirs, theirs, x2s.at[c, src], x2r.at[c, src], tp=2 * src + core)

    def core_hid(c, k):
        at = x_peer(k)
        block = hid.at[c, core * n_x + at]
        return remote(block, block, c2s.at[c, at], c2r.at[c, at], tp=partner)

    def core_hidden(c, k):
        at = x_peer(k)
        block = hid.at[c, (1 - core) * n_x + at]
        return remote(block, block, c2s.at[c, at], c2r.at[c, at], tp=partner)

    acc[...] = jnp.zeros_like(acc)

    def step(s, carry):
        @pl.when(s < nc)
        def _():
            c = s
            load_w(c, 0).wait()
            load_w(c, 1).wait()
            every = xg[...].reshape(m, feats)
            for j in range(2):
                y = jnp.dot(every, wg[c, j], preferred_element_type=F32).astype(BF16)
                part[c, 0, j] = y[: m // 2]
                part[c, 1, j] = y[m // 2 :]
            core_sum(c).start()

        @pl.when((s >= 1) & (s < nc + 1))
        def _():
            c = s - 1
            core_sum(c).wait_recv()
            both = part[c, core].astype(F32) + r1[c].astype(F32)
            both = both.astype(BF16)
            for at in range(n_x):
                s1[c, at] = both[:, at * b : (at + 1) * b]
            for k in range(1, n_x):
                x_sum(c, k).start()

        @pl.when((s >= 3) & (s < nc + 3))
        def _():
            c = s - 3
            for k in range(1, n_x):
                x_summed(c, k).wait_recv()
            both = s1[c, x].astype(F32)
            for k in range(1, n_x):
                both = both + r2[c, x_peer(k)].astype(F32)
            g, u = both[0], both[1]
            hid[c, core * n_x + x] = (g / (1.0 + jnp.exp(-g)) * u).astype(BF16)
            for k in range(1, n_x):
                x_hid(c, k).start()
            core_hid(c, 0).start()

        @pl.when((s >= 4) & (s < nc + 4))
        def _():
            c = s - 4
            for k in range(1, n_x):
                x_hidden(c, k).wait_recv()
                core_hid(c, k).start()

        @pl.when(s >= 5)
        def _():
            c = s - 5
            for k in range(n_x):
                core_hidden(c, k).wait_recv()
            load_d(c).wait()
            acc[...] += jnp.dot(hid[c].reshape(m, w), wd[c], preferred_element_type=F32)

        return carry

    lax.fori_loop(0, nc + 5, step, 0)

    ts[...] = acc[...].astype(BF16).reshape(ts.shape)

    def z_sum(k):
        to = tok_peer(k)
        return remote(ts.at[to], tr.at[t], zs.at[to], zr.at[t], tok=to)

    def z_summed(k):
        src = tok_peer(k)
        return remote(ts.at[src], tr.at[src], zs.at[src], zr.at[src], tok=src)

    def z_all(k):
        to = tok_peer(k)
        return remote(tg.at[t], tg.at[t], bs.at[to], br.at[t], tok=to)

    def z_alled(k):
        src = tok_peer(k)
        return remote(tg.at[src], tg.at[src], bs.at[src], br.at[src], tok=src)

    for k in range(1, n_tok):
        z_sum(k).start()

    def col_copy(d):
        off = (d * win_cols) % feats
        return remote(xg.at[:, :, pl.ds(off, win_cols)], wc, wcs.at[d], wcr, tp=d)

    row_owner = (t * win_rows) // feats
    row_off = pl.multiple_of(lax.rem(t * win_rows, feats), win_rows)

    def row_copy(k):
        to = lax.rem(p + k, n_tp)
        return remote(xg.at[:, :, pl.ds(row_off, win_rows)], wr, wrs.at[k], wrr, tp=to)

    for d in range(n_tp):
        owner = d * win_cols // feats

        @pl.when(p == owner)
        def _(d=d, owner=owner):
            if d == owner:
                off = (d * win_cols) % feats
                wc[...] = xg[:, :, off : off + win_cols]
            else:
                col_copy(d).start()

    @pl.when(p == row_owner)
    def _():
        for k in range(1, n_tp):
            row_copy(k).start()
        wr[...] = xg[:, :, pl.ds(row_off, win_rows)]

    total = acc[pl.ds(pl.multiple_of(t * rows, rows), rows), :]
    for k in range(1, n_tok):
        z_summed(k).wait_recv()
        total = total + tr[tok_peer(k)].astype(F32)
    tg[t] = total.astype(BF16)
    for k in range(1, n_tok):
        z_all(k).start()

    @pl.when((p * win_cols) // feats != p)
    def _():
        col_copy(0).wait_recv()

    @pl.when(p != row_owner)
    def _():
        row_copy(1).wait_recv()

    wrow_ref[...] = wr[...].reshape(wrow_ref.shape)
    wcol_ref[...] = wc[...].reshape(wcol_ref.shape)
    for k in range(1, n_tok):
        z_alled(k).wait_recv()
    tgt_ref[...] = tg[...].reshape(tgt_ref.shape)

    @pl.loop(0, nc)
    def _(c):
        core_sum(c).wait_send()
        core_hid(c, 0).wait_send()
        for k in range(1, n_x):
            x_sum(c, k).wait_send()
            x_hid(c, k).wait_send()
            core_hid(c, k).wait_send()

    for k in range(1, n_tok):
        gather(k).wait_send()
        z_sum(k).wait_send()
        z_all(k).wait_send()
    for d in range(n_tp):
        owner = d * win_cols // feats
        if d != owner:

            @pl.when(p == owner)
            def _(d=d):
                col_copy(d).wait_send()

    @pl.when(p == row_owner)
    def _():
        for k in range(1, n_tp):
            row_copy(k).wait_send()


def span(inputs, gate_weight, up_weight, down_weight, n_tok, n_tp):
    rows, feats = inputs.shape
    half = gate_weight.shape[1]
    outs = down_weight.shape[1]
    m = n_tok * rows
    w = min(CHUNK, half)
    nc = half // w
    n_x = n_tp // 2
    b = m // n_tp
    win_rows, win_cols = WIN // n_tok, WIN // n_tp
    dma = pltpu.SemaphoreType.DMA
    anywhere = pl.BlockSpec(memory_space=pl.ANY)
    vmem = pl.BlockSpec(memory_space=pltpu.VMEM)
    return pl.pallas_call(
        functools.partial(span_kernel, n_tok, n_tp),
        out_shape=(
            jax.ShapeDtypeStruct((m, outs), BF16),
            jax.ShapeDtypeStruct((m, win_rows), BF16),
            jax.ShapeDtypeStruct((m, win_cols), BF16),
        ),
        in_specs=[anywhere] * 4,
        out_specs=(vmem, vmem, vmem),
        scratch_shapes=[
            pltpu.VMEM((n_tok, rows, feats), BF16),
            pltpu.VMEM((nc, 2, feats, w), BF16),
            pltpu.VMEM((nc, w, outs), BF16),
            pltpu.VMEM((nc, 2, 2, m // 2, w), BF16),
            pltpu.VMEM((nc, 2, m // 2, w), BF16),
            pltpu.VMEM((nc, n_x, 2, b, w), BF16),
            pltpu.VMEM((nc, n_x, 2, b, w), BF16),
            pltpu.VMEM((nc, n_tp, b, w), BF16),
            pltpu.VMEM((m, outs), F32),
            pltpu.VMEM((n_tok, rows, outs), BF16),
            pltpu.VMEM((n_tok, rows, outs), BF16),
            pltpu.VMEM((n_tok, rows, outs), BF16),
            pltpu.VMEM((n_tok, rows, win_rows), BF16),
            pltpu.VMEM((n_tok, rows, win_cols), BF16),
            dma(()), dma((nc, 2)), dma((nc,)),
            dma((n_tok,)), dma((n_tok,)),
            dma((nc,)), dma((nc,)),
            dma((nc, n_x)), dma((nc, n_x)),
            dma((nc, n_x)), dma((nc, n_x)),
            dma((nc, n_x)), dma((nc, n_x)),
            dma((n_tok,)), dma((n_tok,)),
            dma((n_tok,)), dma((n_tok,)),
            dma((n_tp,)), dma(()),
            dma((n_tp,)), dma(()),
        ],
        compiler_params=pltpu.CompilerParams(
            collective_id=0, has_side_effects=True, vmem_limit_bytes=58 * 2**20
        ),
        cost_estimate=pl.CostEstimate(
            flops=4 * m * feats * half + 2 * m * half * outs,
            bytes_accessed=2 * (2 * feats * half + half * outs),
            transcendentals=0,
        ),
    )(inputs, gate_weight, up_weight, down_weight)


def shards(n_tok, n_tp, inputs, gate_weight, up_weight, down_weight):
    target, win_rows, win_cols = span(inputs, gate_weight, up_weight, down_weight, n_tok, n_tp)
    gram = jnp.dot(win_rows.T, win_cols, preferred_element_type=F32)
    cross = jnp.dot(win_rows.T, target, preferred_element_type=F32)
    return gram, cross


def solution(mesh):
    placed = (P(("grp", "tok"), "tp"), P("tp", "tok"), P("tp", "tok"), P("tok", "tp"))
    return jax.shard_map(
        functools.partial(shards, mesh.shape["tok"], mesh.shape["tp"]),
        mesh=mesh,
        in_specs=placed,
        out_specs=(P(("grp", "tok"), "tp"), P(("grp", "tok"), "tp")),
        check_vma=False,
    )
```

time: 546 us -> 66.8 us (0.12)
  waiting for transfers between devices: 237 us -> 0 us
  blocking collectives: 203 us -> 0 us
  Pallas kernels: 0 us -> 59.4 us
  matrix products: 34 us -> 6.57 us
  local copies, waits for them, and re-layouts: 26.6 us -> 0.01 us
  other arithmetic: 19.2 us -> 0 us
  between operations: 13.8 us -> 0.66 us
  starting transfers between devices: 11.7 us -> 0 us
    all_gather x2 -> x0, blocking collectives: 203 us -> none  [the longest x1 194 us: shards(): every_token = lax.all_gather(inputs, 'tok', axis=0, tiled=True)]
    all_to_all x2 -> x0, waiting for transfers between devices: 168 us -> none  [the longest x1 168 us: shards(): lax.all_to_all(cross_part, 'tok', split_axis=0, concat_axis=0, tiled=True)]
    pallas_call x0 -> x1, Pallas kernels: none -> 59.4 us  [span(): pl.pallas_call(functools.partial(span_kernel, n_tok, n_tp), out_shape=(ja...]
    reduce_scatter x2 -> x0, waiting for transfers between devices: 52 us -> none  [the longest x1 32.2 us: shards(): lax.psum_scatter(jnp.concatenate([gate_part, up_part], axis=1).astype(jnp...]
    dot_general x5 -> x2, matrix products: 34 us -> 6.57 us  [the longest x1 3.83 us: shards(): gram = jnp.dot(win_rows.T, win_cols, preferred_element_type=F32)]
    all_gather x1 -> x0, waiting for transfers between devices: 16.7 us -> none  [shards(): lax.all_gather(hidden, 'tp', axis=0, tiled=True)]
    all_to_all x2 -> x0, local copies, waits for them, and re-layouts: 15.9 us -> none  [the longest x1 7.94 us: shards(): lax.all_to_all(gram_part, 'tok', split_axis=0, concat_axis=0, tiled=True)]
    reduce_sum x2 -> x0, other arithmetic: 15.8 us -> none  [fold_parts(): received.astype(jnp.float32).reshape(owners, rows, received.shape[1])]
  transfers between devices with their start and end apart: 5 -> 0, of which waited for: 4 -> 0; matrix products, arithmetic and copies ran while one was open for 10% -> 0% of each run, Pallas kernels for 0% -> 0%
where the time goes in v1:
time: 66.8 us; the launch traced here: 66.6 us
  Pallas kernels  59.4 us (89%)
  matrix products  6.57 us (10%)
    pallas_call x1, Pallas kernels, span(): pl.pallas_call(functools.partial(span_kernel, n_tok, n_tp), out_shape=(ja...  59.4 us
    dot_general x1, matrix products, shards(): gram = jnp.dot(win_rows.T, win_cols, preferred_element_type=F32)  3.83 us
    dot_general x1, matrix products, shards(): cross = jnp.dot(win_rows.T, target, preferred_element_type=F32)  2.75 us

profile of v1, /device:TPU:0, one launch (start us, length us, event | category | flops | bytes accessed | tf_op | source)
XLA Modules:
  0.0 66.6 jit_solution(714116403203734197)
XLA Ops:
  0.6 59.4 %shard_map.59 = (bf16[128,1024]{1,0:T(8,128)(2,1)}, bf16[128,1024]{1,0:T(8,128)(2,1)}, bf16[128,1024]{1,0:T(8,128)(2,1)}) custom-call(bf16[32,2048]{1,0:T(8,128)(2,1)} %x_ref.1, bf16[2048,4096]{1,0:T(8,128)(2,1)} %gate_ref.1, bf16[2048,4096]{1,0:T(8,128)(2,1)} %up_ref.1, bf16[4096,1024]{1,0:T(8,128)(2,1)} %down_ref.1), custom_call_target="tpu_custom_call" | custom-call | flops 5368709120 | bytes 41943040 | tf_op jit(solution)/shard_map/pallas_call | solution.py:294
  60.0 0.0 copy-start
  60.0 0.0 copy-start.1
  60.0 3.8 %fusion = f32[1024,1024]{1,0:T(8,128)} fusion(bf16[128,1024]{1,0:T(8,128)(2,1)} %get-tuple-element.5, bf16[128,1024]{1,0:T(8,128)(2,1)} %get-tuple-element.6), kind=kOutput, calls=%fused_computation | convolution fusion | flops 268435456 | bytes 4718592 | tf_op jit(solution)/shard_map/dot_general | solution.py:342
  63.9 0.0 copy-done
  63.9 0.0 copy-done.1
  63.9 2.7 %fusion.1 = f32[1024,1024]{1,0:T(8,128)} fusion(bf16[128,1024]{1,0:T(8,128)(2,1)S(1)} %copy-done, bf16[128,1024]{1,0:T(8,128)(2,1)S(1)} %copy-done.1), kind=kOutput, calls=%fused_computation.1 | convolution fusion | flops 268435456 | bytes 4718592 | tf_op jit(solution)/shard_map/dot_general | solution.py:343
Async XLA Ops:
  60.0 3.8 %copy-start = (bf16[128,1024]{1,0:T(8,128)(2,1)S(1)}, bf16[128,1024]{1,0:T(8,128)(2,1)}, u32[]{:S(2)}) copy-start(bf16[128,1024]{1,0:T(8,128)(2,1)} %get-tuple-element.5) | copy-start | bytes 786436
  60.0 3.8 %copy-start.1 = (bf16[128,1024]{1,0:T(8,128)(2,1)S(1)}, bf16[128,1024]{1,0:T(8,128)(2,1)}, u32[]{:S(2)}) copy-start(bf16[128,1024]{1,0:T(8,128)(2,1)} %get-tuple-element.7) | copy-start | bytes 786436

commit v2 on v1

v2 whole, which is shorter than its diff:
```python
import functools

import jax
import jax.numpy as jnp
from jax import lax
from jax.experimental import pallas as pl
from jax.experimental.pallas import tpu as pltpu
from jax.sharding import PartitionSpec as P

WIN = 4096
CHUNK = 1024
LAGS = (2, 4, 6, 8)
Z_LAG = 3
STAT_ROWS = 256
MESH = pl.DeviceIdType.MESH
F32 = jnp.float32
BF16 = jnp.bfloat16


def span_kernel(
    n_tok, n_tp,
    x_ref, gate_ref, up_ref, down_ref,
    tgt_ref, wrow_ref, wcol_ref,
    xg, wg, wd, part, r1, s1, r2, hid, acc, ts, tr, tg, wr, wc,
    ld_x, ld_w, ld_d, gs, gr, c1s, c1r, x1s, x1r, x2s, x2r, c2s, c2r,
    zs, zr, bs, br, wrs, wrr, wcs, wcr,
):
    t = lax.axis_index("tok")
    p = lax.axis_index("tp")
    core = lax.rem(p, 2)
    x = p // 2
    n_x = n_tp // 2
    nc, _, feats, w = wg.shape
    rows = xg.shape[1]
    m = n_tok * rows // 2
    b = m // n_tp
    sub = rows // 2
    ns = 2 * nc
    early = n_tok // 2
    shift = n_tok // 4
    place = lax.rem(t + n_tok - shift, n_tok)
    win_rows, win_cols = wr.shape[2], wc.shape[2]

    def tok_peer(k):
        return lax.rem(t + k, n_tok)

    def x_peer(k):
        return lax.rem(x + k, n_x)

    def remote(src, dst, ssem, rsem, **where):
        return pltpu.make_async_remote_copy(
            src_ref=src, dst_ref=dst, send_sem=ssem, recv_sem=rsem,
            device_id=where, device_id_type=MESH,
        )

    partner = p + 1 - 2 * core

    own_x = pltpu.make_async_copy(x_ref, xg.at[place], ld_x)
    own_x.start()

    def load_w(c, j):
        src = (gate_ref, up_ref)[j]
        cols = pl.ds(pl.multiple_of(c * w, w), w)
        return pltpu.make_async_copy(src.at[:, cols], wg.at[c, j], ld_w.at[c, j])

    def load_d(c):
        return pltpu.make_async_copy(
            down_ref.at[pl.ds(pl.multiple_of(c * w, w), w), :], wd.at[c], ld_d.at[c]
        )

    @pl.loop(0, nc)
    def _(c):
        load_w(c, 0).start()
        load_w(c, 1).start()

    @pl.loop(0, nc)
    def _(c):
        load_d(c).start()

    barrier = pltpu.get_barrier_semaphore()
    for k in range(1, n_tok):
        pl.semaphore_signal(barrier, inc=1, device_id={"tok": tok_peer(k)}, device_id_type=MESH)
    for k in range(1, n_tp):
        pl.semaphore_signal(barrier, inc=1, device_id={"tp": lax.rem(p + k, n_tp)}, device_id_type=MESH)
    pl.semaphore_wait(barrier, n_tok + n_tp - 2)

    def gather(k):
        to = tok_peer(k)
        return remote(x_ref, xg.at[place], gs.at[to], gr.at[place], tok=to)

    def gathered(at):
        return remote(x_ref, xg.at[at], gs.at[at], gr.at[at], tok=tok_peer(1))

    def send_tokens():
        for k in range(1, n_tok):
            gather(k).start()

    def await_tokens(first, last):
        for at in range(first, last):

            @pl.when(place != at)
            def _(at=at):
                gathered(at).wait_recv()

    @pl.when(place < early)
    def _():
        send_tokens()

    own_x.wait()
    await_tokens(0, early)

    @pl.when(place >= early)
    def _():
        send_tokens()

    def core_sum(c):
        return remote(part.at[c, 1 - core], r1.at[c], c1s.at[c], c1r.at[c], tp=partner)

    def x_sum(c, k):
        to = x_peer(k)
        return remote(s1.at[c, to], r2.at[c, x], x1s.at[c, to], x1r.at[c, x], tp=2 * to + core)

    def x_summed(c, k):
        src = x_peer(k)
        return remote(s1.at[c, src], r2.at[c, src], x1s.at[c, src], x1r.at[c, src], tp=2 * src + core)

    def x_hid(c, k):
        to = x_peer(k)
        mine = hid.at[c, core * n_x + x]
        return remote(mine, mine, x2s.at[c, to], x2r.at[c, x], tp=2 * to + core)

    def x_hidden(c, k):
        src = x_peer(k)
        theirs = hid.at[c, core * n_x + src]
        return remote(theirs, theirs, x2s.at[c, src], x2r.at[c, src], tp=2 * src + core)

    def core_hid(c, k):
        at = x_peer(k)
        block = hid.at[c, core * n_x + at]
        return remote(block, block, c2s.at[c, at], c2r.at[c, at], tp=partner)

    def core_hidden(c, k):
        at = x_peer(k)
        block = hid.at[c, (1 - core) * n_x + at]
        return remote(block, block, c2s.at[c, at], c2r.at[c, at], tp=partner)

    def z_sum(h, k):
        to = tok_peer(k)
        return remote(ts.at[h, to], tr.at[h, t], zs.at[h, to], zr.at[h, t], tok=to)

    def z_summed(h, k):
        src = tok_peer(k)
        return remote(ts.at[h, src], tr.at[h, src], zs.at[h, src], zr.at[h, src], tok=src)

    def z_all(h, k):
        to = tok_peer(k)
        return remote(tg.at[h, t], tg.at[h, t], bs.at[h, to], br.at[h, t], tok=to)

    def z_alled(h, k):
        src = tok_peer(k)
        return remote(tg.at[h, src], tg.at[h, src], bs.at[h, src], br.at[h, src], tok=src)

    def z_send(h):
        ts[h] = acc[h].astype(BF16).reshape(ts.shape[1:])
        for k in range(1, n_tok):
            z_sum(h, k).start()

    def z_reduce(h):
        total = acc[h, pl.ds(pl.multiple_of(t * sub, sub), sub), :]
        for k in range(1, n_tok):
            z_summed(h, k).wait_recv()
            total = total + tr[h, tok_peer(k)].astype(F32)
        tg[h, t] = total.astype(BF16)
        for k in range(1, n_tok):
            z_all(h, k).start()

    def col_copy(d):
        off = (d * win_cols) % feats
        return remote(xg.at[:, :, pl.ds(off, win_cols)], wc, wcs.at[d], wcr, tp=d)

    row_owner = (t * win_rows) // feats
    row_off = pl.multiple_of(lax.rem(t * win_rows, feats), win_rows)

    def row_copy(k):
        to = lax.rem(p + k, n_tp)
        return remote(xg.at[:, :, pl.ds(row_off, win_rows)], wr, wrs.at[k], wrr, tp=to)

    def send_window():
        for d in range(n_tp):
            owner = d * win_cols // feats

            @pl.when(p == owner)
            def _(d=d, owner=owner):
                if d == owner:
                    off = (d * win_cols) % feats
                    wc[...] = xg[:, :, off : off + win_cols]
                else:
                    col_copy(d).start()

        @pl.when(p == row_owner)
        def _():
            for k in range(1, n_tp):
                row_copy(k).start()
            wr[...] = xg[:, :, pl.ds(row_off, win_rows)]

    lag_sum, lag_act, lag_fwd, lag_down = LAGS
    steps = ns + lag_down
    acc[...] = jnp.zeros_like(acc)

    def step(s, carry):
        @pl.when(s == nc)
        def _():
            await_tokens(early, n_tok)

        @pl.when(s < nc)
        def _():
            load_w(s, 0).wait()
            load_w(s, 1).wait()

        @pl.when(s < ns)
        def _():
            c = s
            half, at = c // nc, lax.rem(c, nc)
            tokens = xg[pl.ds(half * early, early)].reshape(m, feats)
            for j in range(2):
                y = jnp.dot(tokens, wg[at, j], preferred_element_type=F32).astype(BF16)
                part[c, 0, j] = y[: m // 2]
                part[c, 1, j] = y[m // 2 :]
            core_sum(c).start()

        @pl.when((s >= lag_sum) & (s < ns + lag_sum))
        def _():
            c = s - lag_sum
            core_sum(c).wait_recv()
            both = part[c, core].astype(F32) + r1[c].astype(F32)
            both = both.astype(BF16)
            for at in range(n_x):
                s1[c, at] = both[:, at * b : (at + 1) * b]
            for k in range(1, n_x):
                x_sum(c, k).start()

        @pl.when((s >= lag_act) & (s < ns + lag_act))
        def _():
            c = s - lag_act
            for k in range(1, n_x):
                x_summed(c, k).wait_recv()
            both = s1[c, x].astype(F32)
            for k in range(1, n_x):
                both = both + r2[c, x_peer(k)].astype(F32)
            g, u = both[0], both[1]
            hid[c, core * n_x + x] = (g / (1.0 + jnp.exp(-g)) * u).astype(BF16)
            for k in range(1, n_x):
                x_hid(c, k).start()
            core_hid(c, 0).start()

        @pl.when(s == ns - 1 + lag_act)
        def _():
            send_window()

        @pl.when((s >= lag_fwd) & (s < ns + lag_fwd))
        def _():
            c = s - lag_fwd
            for k in range(1, n_x):
                x_hidden(c, k).wait_recv()
                core_hid(c, k).start()

        @pl.when(s >= lag_down)
        def _():
            c = s - lag_down
            for k in range(n_x):
                core_hidden(c, k).wait_recv()
            half, at = c // nc, lax.rem(c, nc)

            @pl.when(c < nc)
            def _():
                load_d(c).wait()

            acc[half] += jnp.dot(hid[c].reshape(m, w), wd[at], preferred_element_type=F32)

        @pl.when(s == nc - 1 + lag_down)
        def _():
            z_send(0)

        @pl.when(s == min(nc - 1 + lag_down + Z_LAG, steps - 1))
        def _():
            z_reduce(0)

        return carry

    lax.fori_loop(0, steps, step, 0)
    z_send(1)

    z_reduce(1)

    @pl.when((p * win_cols) // feats != p)
    def _():
        col_copy(0).wait_recv()

    @pl.when(p != row_owner)
    def _():
        row_copy(1).wait_recv()

    wrow_ref[...] = wr[...].reshape(wrow_ref.shape)
    wcol_ref[...] = wc[...].reshape(wcol_ref.shape)
    for h in range(2):
        for k in range(1, n_tok):
            z_alled(h, k).wait_recv()
    tgt_ref[...] = tg[...].reshape(tgt_ref.shape)

    @pl.loop(0, ns)
    def _(c):
        core_sum(c).wait_send()
        core_hid(c, 0).wait_send()
        for k in range(1, n_x):
            x_sum(c, k).wait_send()
            x_hid(c, k).wait_send()
            core_hid(c, k).wait_send()

    for k in range(1, n_tok):
        gather(k).wait_send()
        for h in range(2):
            z_sum(h, k).wait_send()
            z_all(h, k).wait_send()
    for d in range(n_tp):
        owner = d * win_cols // feats
        if d != owner:

            @pl.when(p == owner)
            def _(d=d):
                col_copy(d).wait_send()

    @pl.when(p == row_owner)
    def _():
        for k in range(1, n_tp):
            row_copy(k).wait_send()


def span(inputs, gate_weight, up_weight, down_weight, n_tok, n_tp):
    rows, feats = inputs.shape
    half = gate_weight.shape[1]
    outs = down_weight.shape[1]
    m = n_tok * rows // 2
    sub = rows // 2
    w = min(CHUNK, half)
    nc = half // w
    ns = 2 * nc
    n_x = n_tp // 2
    b = m // n_tp
    win_rows, win_cols = WIN // n_tok, WIN // n_tp
    dma = pltpu.SemaphoreType.DMA
    anywhere = pl.BlockSpec(memory_space=pl.ANY)
    vmem = pl.BlockSpec(memory_space=pltpu.VMEM)
    return pl.pallas_call(
        functools.partial(span_kernel, n_tok, n_tp),
        out_shape=(
            jax.ShapeDtypeStruct((2 * m, outs), BF16),
            jax.ShapeDtypeStruct((2 * m, win_rows), BF16),
            jax.ShapeDtypeStruct((2 * m, win_cols), BF16),
        ),
        in_specs=[anywhere] * 4,
        out_specs=(vmem, vmem, vmem),
        scratch_shapes=[
            pltpu.VMEM((n_tok, rows, feats), BF16),
            pltpu.VMEM((nc, 2, feats, w), BF16),
            pltpu.VMEM((nc, w, outs), BF16),
            pltpu.VMEM((ns, 2, 2, m // 2, w), BF16),
            pltpu.VMEM((ns, 2, m // 2, w), BF16),
            pltpu.VMEM((ns, n_x, 2, b, w), BF16),
            pltpu.VMEM((ns, n_x, 2, b, w), BF16),
            pltpu.VMEM((ns, n_tp, b, w), BF16),
            pltpu.VMEM((2, m, outs), F32),
            pltpu.VMEM((2, n_tok, sub, outs), BF16),
            pltpu.VMEM((2, n_tok, sub, outs), BF16),
            pltpu.VMEM((2, n_tok, sub, outs), BF16),
            pltpu.VMEM((n_tok, rows, win_rows), BF16),
            pltpu.VMEM((n_tok, rows, win_cols), BF16),
            dma(()), dma((nc, 2)), dma((nc,)),
            dma((n_tok,)), dma((n_tok,)),
            dma((ns,)), dma((ns,)),
            dma((ns, n_x)), dma((ns, n_x)),
            dma((ns, n_x)), dma((ns, n_x)),
            dma((ns, n_x)), dma((ns, n_x)),
            dma((2, n_tok)), dma((2, n_tok)),
            dma((2, n_tok)), dma((2, n_tok)),
            dma((n_tp,)), dma(()),
            dma((n_tp,)), dma(()),
        ],
        compiler_params=pltpu.CompilerParams(
            collective_id=0, has_side_effects=True, vmem_limit_bytes=58 * 2**20
        ),
        cost_estimate=pl.CostEstimate(
            flops=8 * m * feats * half + 4 * m * half * outs,
            bytes_accessed=2 * (2 * feats * half + half * outs),
            transcendentals=0,
        ),
    )(inputs, gate_weight, up_weight, down_weight)


def statistics_kernel(rows_ref, cols_ref, tgt_ref, gram_ref, cross_ref):
    turned = rows_ref[...].T
    gram_ref[...] = jnp.dot(turned, cols_ref[...], preferred_element_type=F32)
    cross_ref[...] = jnp.dot(turned, tgt_ref[...], preferred_element_type=F32)


def statistics(win_rows, win_cols, target):
    m, height = win_rows.shape
    width, outs = win_cols.shape[1], target.shape[1]
    tile = min(STAT_ROWS, height)
    whole = lambda n: pl.BlockSpec((m, n), lambda i: (0, 0))
    return pl.pallas_call(
        statistics_kernel,
        out_shape=(
            jax.ShapeDtypeStruct((height, width), F32),
            jax.ShapeDtypeStruct((height, outs), F32),
        ),
        grid=(height // tile,),
        in_specs=[pl.BlockSpec((m, tile), lambda i: (0, i)), whole(width), whole(outs)],
        out_specs=(
            pl.BlockSpec((tile, width), lambda i: (i, 0)),
            pl.BlockSpec((tile, outs), lambda i: (i, 0)),
        ),
        compiler_params=pltpu.CompilerParams(vmem_limit_bytes=32 * 2**20),
        cost_estimate=pl.CostEstimate(
            flops=2 * m * height * (width + outs),
            bytes_accessed=2 * m * (height + width + outs) + 4 * height * (width + outs),
            transcendentals=0,
        ),
    )(win_rows, win_cols, target)


def shards(n_tok, n_tp, inputs, gate_weight, up_weight, down_weight):
    target, win_rows, win_cols = span(inputs, gate_weight, up_weight, down_weight, n_tok, n_tp)
    return statistics(win_rows, win_cols, target)


def solution(mesh):
    placed = (P(("grp", "tok"), "tp"), P("tp", "tok"), P("tp", "tok"), P("tok", "tp"))
    return jax.shard_map(
        functools.partial(shards, mesh.shape["tok"], mesh.shape["tp"]),
        mesh=mesh,
        in_specs=placed,
        out_specs=(P(("grp", "tok"), "tp"), P(("grp", "tok"), "tp")),
        check_vma=False,
    )
```

time: 66.8 us -> 64.7 us (0.969)
  matrix products: 6.57 us -> 0 us
  local copies, waits for them, and re-layouts: 0.01 us -> 2.84 us
  Pallas kernels: 59.4 us -> 61 us
    dot_general x2 -> x0, matrix products: 6.57 us -> none  [the longest x1 3.83 us: shards(): gram = jnp.dot(win_rows.T, win_cols, preferred_element_type=F32)]
    pallas_call x0 -> x1, Pallas kernels: none -> 3.97 us  [statistics(): pl.pallas_call(statistics_kernel, out_shape=(jax.ShapeDtypeStruct((height...]
    unnamed x4 -> x6, local copies, waits for them, and re-layouts: 0.01 us -> 2.84 us
    pallas_call x1, Pallas kernels: 59.4 us -> 57 us  [span(): pl.pallas_call(functools.partial(span_kernel, n_tok, n_tp), out_shape=(ja...]
where the time goes in v2:
time: 64.7 us; the launch traced here: 64.4 us
  Pallas kernels  61 us (94%)
  local copies, waits for them, and re-layouts  2.84 us (4%)
  between operations  0.65 us (1%)
    pallas_call x1, Pallas kernels, span(): pl.pallas_call(functools.partial(span_kernel, n_tok, n_tp), out_shape=(ja...  57 us
    pallas_call x1, Pallas kernels, statistics(): pl.pallas_call(statistics_kernel, out_shape=(jax.ShapeDtypeStruct((height...  3.97 us
    unnamed x6, local copies, waits for them, and re-layouts  2.84 us

profile of v2, /device:TPU:0, one launch (start us, length us, event | category | flops | bytes accessed | tf_op | source)
XLA Modules:
  0.0 64.4 jit_solution(17587631634765060150)
XLA Ops:
  0.6 57.0 %shard_map.59 = (bf16[128,1024]{1,0:T(8,128)(2,1)}, bf16[128,1024]{1,0:T(8,128)(2,1)}, bf16[128,1024]{1,0:T(8,128)(2,1)}) custom-call(bf16[32,2048]{1,0:T(8,128)(2,1)} %x_ref.1, bf16[2048,4096]{1,0:T(8,128)(2,1)} %gate_ref.1, bf16[2048,4096]{1,0:T(8,128)(2,1)} %up_ref.1, bf16[4096,1024]{1,0:T(8,128)(2,1)} %down_ref.1), custom_call_target="tpu_custom_call" | custom-call | flops 5368709120 | bytes 41943040 | tf_op jit(solution)/shard_map/pallas_call | solution.py:353
  57.6 0.0 copy-start
  57.6 0.9 %copy-done = bf16[128,1024]{1,0:T(8,128)(2,1)S(1)} copy-done((bf16[128,1024]{1,0:T(8,128)(2,1)S(1)}, bf16[128,1024]{1,0:T(8,128)(2,1)}, u32[]{:S(2)}) %copy-start) | copy-done | bytes 262168
  58.6 0.0 copy-start.1
  58.6 0.9 %copy-done.1 = bf16[128,1024]{1,0:T(8,128)(2,1)S(1)} copy-done((bf16[128,1024]{1,0:T(8,128)(2,1)S(1)}, bf16[128,1024]{1,0:T(8,128)(2,1)}, u32[]{:S(2)}) %copy-start.1) | copy-done | bytes 262168
  59.5 0.0 copy-start.2
  59.5 0.9 %copy-done.2 = bf16[128,1024]{1,0:T(8,128)(2,1)S(1)} copy-done((bf16[128,1024]{1,0:T(8,128)(2,1)S(1)}, bf16[128,1024]{1,0:T(8,128)(2,1)}, u32[]{:S(2)}) %copy-start.2) | copy-done | bytes 262168
  60.5 4.0 %shard_map.60 = (f32[1024,1024]{1,0:T(8,128)}, f32[1024,1024]{1,0:T(8,128)}) custom-call(bf16[128,1024]{1,0:T(8,128)(2,1)S(1)} %copy-done.1, bf16[128,1024]{1,0:T(8,128)(2,1)S(1)} %copy-done.2, bf16[128,1024]{1,0:T(8,128)(2,1)S(1)} %copy-done), custom_call_target="tpu_custom_call" | custom-call | flops 536870912 | bytes 9175040 | tf_op jit(solution)/shard_map/pallas_call | solution.py:410
Async XLA Ops:
  57.6 1.0 %copy-start = (bf16[128,1024]{1,0:T(8,128)(2,1)S(1)}, bf16[128,1024]{1,0:T(8,128)(2,1)}, u32[]{:S(2)}) copy-start(bf16[128,1024]{1,0:T(8,128)(2,1)} %get-tuple-element.7.tgt_ref) | copy-start | bytes 786436
  58.6 0.9 %copy-start.1 = (bf16[128,1024]{1,0:T(8,128)(2,1)S(1)}, bf16[128,1024]{1,0:T(8,128)(2,1)}, u32[]{:S(2)}) copy-start(bf16[128,1024]{1,0:T(8,128)(2,1)} %get-tuple-element.5.rows_ref) | copy-start | bytes 786436
  59.5 0.9 %copy-start.2 = (bf16[128,1024]{1,0:T(8,128)(2,1)S(1)}, bf16[128,1024]{1,0:T(8,128)(2,1)}, u32[]{:S(2)}) copy-start(bf16[128,1024]{1,0:T(8,128)(2,1)} %get-tuple-element.6.cols_ref) | copy-start | bytes 786436

commit v3 on v2

--- a/solution.py
+++ b/solution.py
@@ -9,7 +9,7 @@
 
 WIN = 4096
 CHUNK = 1024
-LAGS = (2, 4, 6, 8)
+LAGS = (1,2,3,4)
 Z_LAG = 3
 STAT_ROWS = 256
 MESH = pl.DeviceIdType.MESH
@@ -419,7 +419,7 @@
             pl.BlockSpec((tile, width), lambda i: (i, 0)),
             pl.BlockSpec((tile, outs), lambda i: (i, 0)),
         ),
-        compiler_params=pltpu.CompilerParams(vmem_limit_bytes=32 * 2**20),
+        compiler_params=pltpu.CompilerParams(vmem_limit_bytes=58 * 2**20),
         cost_estimate=pl.CostEstimate(
             flops=2 * m * height * (width + outs),
             bytes_accessed=2 * m * (height + width + outs) + 4 * height * (width + outs),

time: 64.7 us -> 61.3 us (0.947)
  local copies, waits for them, and re-layouts: 2.84 us -> 0 us
    unnamed x6 -> x0, local copies, waits for them, and re-layouts: 2.84 us -> none
    pallas_call x1, Pallas kernels: 57 us -> 55.2 us  [span(): pl.pallas_call(functools.partial(span_kernel, n_tok, n_tp), out_shape=(ja...]
    pallas_call x1, Pallas kernels: 3.97 us -> 5.24 us  [statistics(): pl.pallas_call(statistics_kernel, out_shape=(jax.ShapeDtypeStruct((height...]
where the time goes in v3:
time: 61.3 us; the launch traced here: 61.1 us
  Pallas kernels  60.4 us (99%)
  between operations  0.64 us (1%)
    pallas_call x1, Pallas kernels, span(): pl.pallas_call(functools.partial(span_kernel, n_tok, n_tp), out_shape=(ja...  55.2 us
    pallas_call x1, Pallas kernels, statistics(): pl.pallas_call(statistics_kernel, out_shape=(jax.ShapeDtypeStruct((height...  5.24 us

profile of v3, /device:TPU:0, one launch (start us, length us, event | category | flops | bytes accessed | tf_op | source)
XLA Modules:
  0.0 61.1 jit_solution(4286727204245761755)
XLA Ops:
  0.6 55.2 %shard_map.59 = (bf16[128,1024]{1,0:T(8,128)(2,1)}, bf16[128,1024]{1,0:T(8,128)(2,1)}, bf16[128,1024]{1,0:T(8,128)(2,1)}) custom-call(bf16[32,2048]{1,0:T(8,128)(2,1)} %x_ref.1, bf16[2048,4096]{1,0:T(8,128)(2,1)} %gate_ref.1, bf16[2048,4096]{1,0:T(8,128)(2,1)} %up_ref.1, bf16[4096,1024]{1,0:T(8,128)(2,1)} %down_ref.1), custom_call_target="tpu_custom_call" | custom-call | flops 5368709120 | bytes 41943040 | tf_op jit(solution)/shard_map/pallas_call | solution.py:353
  55.8 5.2 %shard_map.60 = (f32[1024,1024]{1,0:T(8,128)}, f32[1024,1024]{1,0:T(8,128)}) custom-call(bf16[128,1024]{1,0:T(8,128)(2,1)} %get-tuple-element.5.rows_ref, bf16[128,1024]{1,0:T(8,128)(2,1)} %get-tuple-element.6.cols_ref, bf16[128,1024]{1,0:T(8,128)(2,1)} %get-tuple-element.7.tgt_ref), custom_call_target="tpu_custom_call" | custom-call | flops 536870912 | bytes 9175040 | tf_op jit(solution)/shard_map/pallas_call | solution.py:410

commit v4 on v3

--- a/solution.py
+++ b/solution.py
@@ -11,7 +11,7 @@
 CHUNK = 1024
 LAGS = (1,2,3,4)
 Z_LAG = 3
-STAT_ROWS = 256
+STAT_ROWS = 128
 MESH = pl.DeviceIdType.MESH
 F32 = jnp.float32
 BF16 = jnp.bfloat16

time: 61.3 us -> 63 us (1.028)
  Pallas kernels: 60.4 us -> 61.9 us
    pallas_call x1, Pallas kernels: 5.24 us -> 6.73 us  [statistics(): pl.pallas_call(statistics_kernel, out_shape=(jax.ShapeDtypeStruct((height...]
where the time goes in v4:
time: 63 us; the launch traced here: 62.5 us
  Pallas kernels  61.9 us (98%)
  between operations  0.64 us (1%)
    pallas_call x1, Pallas kernels, span(): pl.pallas_call(functools.partial(span_kernel, n_tok, n_tp), out_shape=(ja...  55.2 us
    pallas_call x1, Pallas kernels, statistics(): pl.pallas_call(statistics_kernel, out_shape=(jax.ShapeDtypeStruct((height...  6.73 us

profile of v4, /device:TPU:0, one launch (start us, length us, event | category | flops | bytes accessed | tf_op | source)
XLA Modules:
  0.0 62.5 jit_solution(14257086546205194467)
XLA Ops:
  0.6 55.2 %shard_map.59 = (bf16[128,1024]{1,0:T(8,128)(2,1)}, bf16[128,1024]{1,0:T(8,128)(2,1)}, bf16[128,1024]{1,0:T(8,128)(2,1)}) custom-call(bf16[32,2048]{1,0:T(8,128)(2,1)} %x_ref.1, bf16[2048,4096]{1,0:T(8,128)(2,1)} %gate_ref.1, bf16[2048,4096]{1,0:T(8,128)(2,1)} %up_ref.1, bf16[4096,1024]{1,0:T(8,128)(2,1)} %down_ref.1), custom_call_target="tpu_custom_call" | custom-call | flops 5368709120 | bytes 41943040 | tf_op jit(solution)/shard_map/pallas_call | solution.py:353
  55.8 6.7 %shard_map.60 = (f32[1024,1024]{1,0:T(8,128)}, f32[1024,1024]{1,0:T(8,128)}) custom-call(bf16[128,1024]{1,0:T(8,128)(2,1)} %get-tuple-element.5.rows_ref, bf16[128,1024]{1,0:T(8,128)(2,1)} %get-tuple-element.6.cols_ref, bf16[128,1024]{1,0:T(8,128)(2,1)} %get-tuple-element.7.tgt_ref), custom_call_target="tpu_custom_call" | custom-call | flops 536870912 | bytes 9175040 | tf_op jit(solution)/shard_map/pallas_call | solution.py:410
